TPU v7x, 32 devices: a whole 2x2x4 slice. The times are simulated.
32 devices in a mesh: kgrp: 8 (over y, x, core), pts: 4 (over z).
Axes of the slice: x: 2, y: 2, z: 4, core: 2. Of those that a mesh axis runs over, the one named last changes fastest.
Arguments:
- vectors: bfloat16 [32, 32, 2048], P('kgrp'), may hold values from -6 to 6
- psi_val: bfloat16 [32, 48, 2048], P('kgrp', None, 'pts'), may hold values from -1.1953125 to 1.1953125
- psi_con: bfloat16 [32, 96, 2048], P('kgrp', None, 'pts'), may hold values from -1.1953125 to 1.1953125
- val_count: int32 [32], P('kgrp'), may hold values from 8 to 32, as said below
- con_count: int32 [32], P('kgrp'), may hold values from 16 to 64, as said below
- val_offset: int32 [32], P('kgrp'), may hold values from 0 to 16
- con_offset: int32 [32], P('kgrp'), may hold values from 0 to 32
- screening: bfloat16 [32, 2048, 2048], P('kgrp', 'pts'), may hold values from -0.0234375 to 0.0234375
- q_table: int32 [32, 32], replicated, may hold values from 0 to 31, as said below
Outputs:
- kernel_image: bfloat16 [32, 32, 2048], P('kgrp', None, 'pts')
Inputs may be any that keep to these rules, and one draw needn't show every extreme that they name: `val_count`: at least one k-point has a full window of 32 valence bands. `con_count`: at least one k-point has a full window of 64 conduction bands. q_table[k, k'] = (label_k - label_k') mod 32 for a permutation label of 0 to 31, so every row and every column holds each q once.
All inputs are finite; a program needn't handle non-finite values.
Results may differ from a plain program's by a relative error of at most 0.023.
Values may be sent and summed in bfloat16 or wider, within the bound.
A program may use at most 64 MiB of HBM per device.

v0:
```python
import jax
import jax.numpy as jnp
from jax import lax
from jax.sharding import PartitionSpec as P

NV = 32
NC = 64


def pair_window(psi_v, psi_c, count_v, count_c, start_v, start_c):
    win_v = lax.dynamic_slice_in_dim(psi_v, start_v, NV, 0).astype(jnp.float32)
    win_c = lax.dynamic_slice_in_dim(psi_c, start_c, NC, 0).astype(jnp.float32)
    keep_v = (jnp.arange(NV, dtype=jnp.int32) < count_v).astype(jnp.float32)
    keep_c = (jnp.arange(NC, dtype=jnp.int32) < count_c).astype(jnp.float32)
    left = win_v * keep_v[:, None]
    right = win_c * keep_c[:, None]
    prod = left[:, None, :] * right[None, :, :]
    return prod.reshape(NV * NC, prod.shape[-1]).astype(jnp.bfloat16)


def shards(
    vectors, psi_val, psi_con, val_count, con_count, val_offset, con_offset, screening, q_table
):
    zeta = jax.vmap(pair_window)(psi_val, psi_con, val_count, con_count, val_offset, con_offset)
    local = jnp.einsum("kbp,kpm->kbm", vectors, zeta, preferred_element_type=jnp.float32).astype(
        jnp.bfloat16
    )
    k_local = local.shape[0]
    k_total = q_table.shape[0]
    m_local = local.shape[2]
    owned = lax.axis_index("kgrp") * k_local + jnp.arange(k_local, dtype=jnp.int32)
    spread = lax.all_gather(local, "pts", axis=2, tiled=True)
    empty = jnp.zeros((k_total, local.shape[1], m_local), jnp.float32)
    piece = lax.all_gather(spread, "kgrp", axis=0, tiled=True)
    width = piece.shape[0]
    positions = jnp.arange(width, dtype=jnp.int32)

    def one_transfer(total, q_entry):
        target, q_block = q_entry
        matching_entry = (q_table == target).astype(jnp.int32)
        found = jnp.sum(matching_entry, axis=1)
        sender_kpoint = jnp.sum(matching_entry * positions[None, :], axis=1)
        picked = jnp.take(piece, sender_kpoint, axis=0) * found.astype(piece.dtype)[:, None, None]
        update = jnp.einsum("cbv,mv->cbm", picked, q_block, preferred_element_type=jnp.float32)
        return (total + update, None)

    summed, unused_slot = lax.scan(one_transfer, empty, (owned, screening))
    home = lax.psum_scatter(summed.astype(jnp.bfloat16), "kgrp", scatter_dimension=0, tiled=True)
    return_trip = jnp.einsum("kbm,kpm->kbp", home, zeta, preferred_element_type=jnp.float32)
    return lax.psum_scatter(
        return_trip.astype(jnp.bfloat16), "pts", scatter_dimension=2, tiled=True
    )


def solution(mesh):
    placed = (
        P("kgrp", None, None),
        P("kgrp", None, "pts"),
        P("kgrp", None, "pts"),
        P("kgrp"),
        P("kgrp"),
        P("kgrp"),
        P("kgrp"),
        P("kgrp", "pts", None),
        P(),
    )
    return jax.shard_map(
        shards, mesh=mesh, in_specs=placed, out_specs=P("kgrp", None, "pts"), check_vma=False
    )
```

profile of v0, /device:TPU:0, one launch (start us, length us, event | category | flops | bytes accessed | tf_op | source)
XLA Modules:
  0.0 195.6 jit_solution(3106491809026536364)
XLA Ops:
  6.6 1.4 copy.16
  8.0 0.7 fusion.29
  8.6 0.7 fusion.19
  9.3 1.8 gather_fusion.2
  11.2 0.2 copy.17
  11.6 1.2 gather_fusion.1
  13.0 3.3 %multiply_convert_fusion = bf16[4,32,64,512]{3,2,1,0:T(8,128)(2,1)S(1)} fusion(f32[4,64,512]{2,1,0:T(8,128)S(1)} %copy.17, f32[4,32,512]{2,1,0:T(8,128)S(1)} %copy.15), kind=kLoop, calls=%fused_computation.24 | loop fusion | flops 8388608 | bytes 9175040 | tf_op jit(solution)/shard_map/vmap()/convert_element_type | solution.py:18
  16.3 1.5 fusion.18
  17.8 1.7 copy-done.1
  19.5 18.0 %all_gather.6 = bf16[4,32,2048]{2,1,0:T(8,128)(2,1)} all-gather(bf16[4,32,512]{2,1,0:T(8,128)(2,1)S(1)} %fusion.18), channel_id=1, replica_groups=mesh['kgrp'=8,'pts'=4] {'pts'}, dimensions={2}, use_global_device_ids=true | all-gather | bytes 655360 | tf_op jit(solution)/shard_map/all_gather | solution.py:32
  37.6 38.7 %all-gather.2.cloned.1.call-done = bf16[32,32,2048]{2,1,0:T(8,128)(2,1)} async-done(((bf16[4,32,2048]{2,1,0:T(8,128)(2,1)}), bf16[32,32,2048]{2,1,0:T(8,128)(2,1)}) %all-gather.2.cloned.1.call-update) | async-done | bytes 4194320 | tf_op jit(solution)/shard_map/all_gather | solution.py:34
  76.3 46.8 %while.11 = (s32[]{:T(128)}, f32[32,32,512]{2,1,0:T(8,128)S(1)}, s32[4]{0:T(128)S(1)}, s32[32,32]{1,0:T(8,128)S(1)}, bf16[32,32,2048]{2,1,0:T(8,128)(2,1)}, /*in...) while((s32[]{:T(128)}, f32[32,32,512]{2,1,0:T(8,128)S(1)}, s32[4]{0:T(128)S(1)}, ...), condition=%wide.region_3.4_spmd.clone, body=%wide.region_0.3_spmd.clone.sunk | while | flops 2152732928 | bytes 18884400 | solution.py:47
  76.3 0.6 dynamic_slice.19
  76.8 0.7 convert_reduce_fusion.2
  77.5 4.9 %gather_fusion = bf16[32,32,2048]{2,1,0:T(8,128)(2,1)} fusion(bf16[32,32,2048]{2,1,0:T(8,128)(2,1)} %get-tuple-element.141, s32[1024]{0:T(1024)S(1)} %pad_clamp_fusion.2), kind=kCustom, calls=%fused_computation.clone.clone.1 | custom fusion | bytes 8388736 | tf_op jit(solution)/shard_map/while/body/eval_jaxpr/jit(_take)/gather | solution.py:43
  82.5 5.5 %select_add_fusion.2 = f32[32,32,512]{2,1,0:T(8,128)S(1)} fusion(f32[32,32,512]{2,1,0:T(8,128)S(1)} %get-tuple-element.130, bf16[4,512,2048]{2,1,0:T(8,128)(2,1)} %get-tuple-element.142, s32[]{:T(128)} %get-tuple-element.129, bf16[32,32,2048]{2,1,0:T(8,128)(2,1)} %gather_fusion, pred[32]{0:T(512)(128)(4,1)S(1)} %compare_and_fusion.2, ...), kind=kOutput, calls=%fused_computation.9.clone.1 | convolution fusion | flops 2152726528 | bytes 10486369 | tf_op jit(solution)/shard_map/while/body/eval_jaxpr/cbv,mv->cbm/dot_general | solution.py:44
  88.0 0.6 dynamic_slice.19
  88.5 0.7 convert_reduce_fusion.2
  89.2 4.9 %gather_fusion = bf16[32,32,2048]{2,1,0:T(8,128)(2,1)} fusion(bf16[32,32,2048]{2,1,0:T(8,128)(2,1)} %get-tuple-element.141, s32[1024]{0:T(1024)S(1)} %pad_clamp_fusion.2), kind=kCustom, calls=%fused_computation.clone.clone.1 | custom fusion | bytes 8388736 | tf_op jit(solution)/shard_map/while/body/eval_jaxpr/jit(_take)/gather | solution.py:43
  94.2 5.5 %select_add_fusion.2 = f32[32,32,512]{2,1,0:T(8,128)S(1)} fusion(f32[32,32,512]{2,1,0:T(8,128)S(1)} %get-tuple-element.130, bf16[4,512,2048]{2,1,0:T(8,128)(2,1)} %get-tuple-element.142, s32[]{:T(128)} %get-tuple-element.129, bf16[32,32,2048]{2,1,0:T(8,128)(2,1)} %gather_fusion, pred[32]{0:T(512)(128)(4,1)S(1)} %compare_and_fusion.2, ...), kind=kOutput, calls=%fused_computation.9.clone.1 | convolution fusion | flops 2152726528 | bytes 10486369 | tf_op jit(solution)/shard_map/while/body/eval_jaxpr/cbv,mv->cbm/dot_general | solution.py:44
  99.7 0.6 dynamic_slice.19
  100.2 0.7 convert_reduce_fusion.2
  100.9 4.9 %gather_fusion = bf16[32,32,2048]{2,1,0:T(8,128)(2,1)} fusion(bf16[32,32,2048]{2,1,0:T(8,128)(2,1)} %get-tuple-element.141, s32[1024]{0:T(1024)S(1)} %pad_clamp_fusion.2), kind=kCustom, calls=%fused_computation.clone.clone.1 | custom fusion | bytes 8388736 | tf_op jit(solution)/shard_map/while/body/eval_jaxpr/jit(_take)/gather | solution.py:43
  105.9 5.5 %select_add_fusion.2 = f32[32,32,512]{2,1,0:T(8,128)S(1)} fusion(f32[32,32,512]{2,1,0:T(8,128)S(1)} %get-tuple-element.130, bf16[4,512,2048]{2,1,0:T(8,128)(2,1)} %get-tuple-element.142, s32[]{:T(128)} %get-tuple-element.129, bf16[32,32,2048]{2,1,0:T(8,128)(2,1)} %gather_fusion, pred[32]{0:T(512)(128)(4,1)S(1)} %compare_and_fusion.2, ...), kind=kOutput, calls=%fused_computation.9.clone.1 | convolution fusion | flops 2152726528 | bytes 10486369 | tf_op jit(solution)/shard_map/while/body/eval_jaxpr/cbv,mv->cbm/dot_general | solution.py:44
  111.4 0.6 dynamic_slice.19
  111.9 0.7 convert_reduce_fusion.2
  112.6 4.9 %gather_fusion = bf16[32,32,2048]{2,1,0:T(8,128)(2,1)} fusion(bf16[32,32,2048]{2,1,0:T(8,128)(2,1)} %get-tuple-element.141, s32[1024]{0:T(1024)S(1)} %pad_clamp_fusion.2), kind=kCustom, calls=%fused_computation.clone.clone.1 | custom fusion | bytes 8388736 | tf_op jit(solution)/shard_map/while/body/eval_jaxpr/jit(_take)/gather | solution.py:43
  117.6 5.5 %select_add_fusion.2 = f32[32,32,512]{2,1,0:T(8,128)S(1)} fusion(f32[32,32,512]{2,1,0:T(8,128)S(1)} %get-tuple-element.130, bf16[4,512,2048]{2,1,0:T(8,128)(2,1)} %get-tuple-element.142, s32[]{:T(128)} %get-tuple-element.129, bf16[32,32,2048]{2,1,0:T(8,128)(2,1)} %gather_fusion, pred[32]{0:T(512)(128)(4,1)S(1)} %compare_and_fusion.2, ...), kind=kOutput, calls=%fused_computation.9.clone.1 | convolution fusion | flops 2152726528 | bytes 10486369 | tf_op jit(solution)/shard_map/while/body/eval_jaxpr/cbv,mv->cbm/dot_general | solution.py:44
  123.1 1.2 convert_element_type.64
  124.3 36.1 %reduce-scatter.3.cloned.1.call-done = bf16[4,32,512]{2,1,0:T(8,128)(2,1)} async-done(((bf16[32,32,512]{2,1,0:T(8,128)(2,1)}), bf16[4,32,512]{2,1,0:T(8,128)(2,1)}) %reduce-scatter.3.cloned.1.call-update) | async-done | bytes 131088 | tf_op jit(solution)/shard_map/reduce_scatter | solution.py:48
  160.5 6.8 %convolution_convert_fusion = bf16[4,32,2048]{2,1,0:T(8,128)(2,1)} fusion(bf16[4,32,512]{2,1,0:T(8,128)(2,1)} %reduce-scatter.3.cloned.1.call-done, bf16[4,2048,512]{2,1,0:T(8,128)(2,1)} %bitcast.43), kind=kOutput, calls=%fused_computation.25 | convolution fusion | flops 268697600 | bytes 9043968 | tf_op jit(solution)/shard_map/kbm,kpm->kbp/dot_general | solution.py:49
  167.3 21.8 %reduce-scatter.5.cloned.1.call-done = bf16[4,32,512]{2,1,0:T(8,128)(2,1)} async-done(((bf16[4,32,2048]{2,1,0:T(8,128)(2,1)}), bf16[4,32,512]{2,1,0:T(8,128)(2,1)}) %reduce-scatter.5.cloned.1.call-update) | async-done | bytes 131088 | tf_op jit(solution)/shard_map/reduce_scatter | solution.py:50
  (41 shorter events, 0.8 us)
Async XLA Ops:
  6.5 9.8 %copy-start = (bf16[4,32,2048]{2,1,0:T(8,128)(2,1)S(1)}, bf16[4,32,2048]{2,1,0:T(8,128)(2,1)}, u32[]{:S(2)}) copy-start(bf16[4,32,2048]{2,1,0:T(8,128)(2,1)} %param.11) | copy-start | bytes 1572868
  6.5 4.9 %copy-start.3 = (bf16[4,48,512]{2,1,0:T(8,128)(2,1)S(1)}, bf16[4,48,512]{2,1,0:T(8,128)(2,1)}, u32[]{:S(2)}) copy-start(bf16[4,48,512]{2,1,0:T(8,128)(2,1)} %param.12) | copy-start | bytes 589828
  6.5 5.0 %copy-start.5 = (s32[4]{0:T(128)S(1)}, s32[4]{0:T(128)}, u32[]{:S(2)}) copy-start(s32[4]{0:T(128)} %param.16) | copy-start | bytes 52
  6.5 5.1 %copy-start.4 = (s32[4]{0:T(128)S(1)}, s32[4]{0:T(128)}, u32[]{:S(2)}) copy-start(s32[4]{0:T(128)} %param.14) | copy-start | bytes 52
  6.5 69.7 %all-gather.2.cloned.1.call-start = ((), (), s32[]{:S(2)}) async-start(), calls=%async_computation.2 | async-start | bytes 4718592 | tf_op jit(solution)/shard_map/all_gather | solution.py:34
  16.3 3.2 %copy-start.1 = (bf16[4,32,64,512]{3,2,1,0:T(8,128)(2,1)}, bf16[4,32,64,512]{3,2,1,0:T(8,128)(2,1)S(1)}, u32[]{:S(2)}) copy-start(bf16[4,32,64,512]{3,2,1,0:T(8,128)(2,1)S(1)} %multiply_convert_fusion) | copy-start | bytes 25165828
  16.3 60.0 %copy-start.2 = (s32[32,32]{1,0:T(8,128)S(1)}, s32[32,32]{1,0:T(8,128)}, u32[]{:S(2)}) copy-start(s32[32,32]{1,0:T(8,128)} %param.19) | copy-start | bytes 12292
  37.5 123.0 %reduce-scatter.3.cloned.1.call-start = ((), (), s32[]{:S(2)}) async-start(), calls=%async_computation.3 | async-start | bytes 1179648 | tf_op jit(solution)/shard_map/reduce_scatter | solution.py:48
  124.3 64.8 %reduce-scatter.5.cloned.1.call-start = ((), (), s32[]{:S(2)}) async-start(), calls=%async_computation.4 | async-start | bytes 655360 | tf_op jit(solution)/shard_map/reduce_scatter | solution.py:50
Sparse Core Ops, SparseCore 0:
  37.6 38.5 all-gather.1
  124.4 36.0 reduce-scatter.2
  167.4 21.6 reduce-scatter.4
where the time goes:
time: 196 us
  waiting for transfers between devices  96.6 us (49%)
  matrix products  30.2 us (15%)
  local copies, waits for them, and re-layouts  28.5 us (15%)
  blocking collectives  18 us (9%)
  between operations  13.3 us (7%)
  other arithmetic  8.77 us (4%)
    all_gather x1, waiting for transfers between devices, shards(): piece = lax.all_gather(spread, 'kgrp', axis=0, tiled=True)  38.7 us
    reduce_scatter x1, waiting for transfers between devices, shards(): lax.psum_scatter(summed.astype(jnp.bfloat16), 'kgrp', scatter_dimension=0...  36.1 us
    dot_general x4, matrix products, one_transfer(): jnp.einsum('cbv,mv->cbm', picked, q_block, preferred_element_type=jnp.flo...  21.9 us
    reduce_scatter x1, waiting for transfers between devices, shards(): lax.psum_scatter(return_trip.astype(jnp.bfloat16), 'pts', scatter_dimensi...  21.8 us
    gather x4, local copies, waits for them, and re-layouts, one_transfer(): jnp.take(piece, sender_kpoint, axis=0)  19.8 us
    all_gather x1, blocking collectives, shards(): spread = lax.all_gather(local, 'pts', axis=2, tiled=True)  18 us
    dot_general x1, matrix products, shards(): jnp.einsum('kbm,kpm->kbp', home, zeta, preferred_element_type=jnp.float32)  6.84 us
  transfers between devices with their start and end apart: 3, of which 3 were waited for; matrix products, arithmetic and copies ran while one was open for 0% of the time, Pallas kernels for 0%

commit v1 on v0

v1 whole, which is shorter than its diff:
```python
import functools

import jax
import jax.numpy as jnp
from jax import lax
from jax.experimental import pallas as pl
from jax.experimental.pallas import tpu as pltpu
from jax.sharding import PartitionSpec as P

NV = 32
NC = 64
MESH = pl.DeviceIdType.MESH
VMEM_BYTES = 60 * 1024 * 1024


def flip(o, d):
    out, bit = o, 1
    while bit <= d:
        if d & bit:
            out = out + bit - 2 * bit * ((o // bit) % 2)
        bit *= 2
    return out


def last_hop(d, i, count):
    low = d & -d
    high = 1 << (d.bit_length() - 1)
    return low if 2 * i < count else high


def nearest(z, i, count):
    far = (2 * z) // count
    zz = z + far * (count - 1 - 2 * z)
    step = (i + 1) // 2
    t = jnp.where(i <= 2 * zz, zz + (step if i % 2 else -step), i)
    return t + far * (count - 1 - 2 * t)


def kernel(
    groups, points,
    val_count, con_count, val_offset, con_offset, sender,
    vectors, psi_val, psi_con, screening, out,
    w_buf, zeta, piece, res, s1, r1, s2, r2, mine, s3, r3, mine3,
    w_sem, ag_send, ag_recv, s1_send, s1_recv, s2_send, s2_recv, s3_send, s3_recv,
):
    k_local, trials, slots = vectors.shape
    m_local = psi_val.shape[2]
    q_local = w_buf.shape[0]
    rows = k_local * trials
    outer = groups // 2
    p_local = slots // points
    g = lax.axis_index("kgrp")
    z = lax.axis_index("pts")
    o, c = g // 2, g % 2
    sibling = g + 1 - 2 * c

    barrier = pltpu.get_barrier_semaphore()
    partners = [(sibling, z)]
    partners += [(flip(o, d) * 2 + c, z) for d in range(1, outer)]
    partners += [(g, (z + t) % points) for t in range(1, points)]
    for who in partners:
        pl.semaphore_signal(barrier, inc=1, device_id=who, device_id_type=MESH)

    w_copy = pltpu.make_async_copy(screening, w_buf, w_sem)
    w_copy.start()

    my_rows = pl.multiple_of(g * rows, rows)

    def project(j, carry):
        def select(count, offset, n, held):
            at = lax.broadcasted_iota(jnp.int32, (n, held), 0)
            src = lax.broadcasted_iota(jnp.int32, (n, held), 1)
            hit = (src == at + offset) & (at < count)
            return jnp.where(hit, 1.0, 0.0).astype(jnp.bfloat16)

        left = jnp.dot(
            select(val_count[j], val_offset[j], NV, psi_val.shape[1]), psi_val[j],
            preferred_element_type=jnp.float32,
        )
        right = jnp.dot(
            select(con_count[j], con_offset[j], NC, psi_con.shape[1]), psi_con[j],
            preferred_element_type=jnp.float32,
        )
        for v in range(NV):
            zeta[j, v * NC : (v + 1) * NC, :] = (left[v : v + 1, :] * right).astype(jnp.bfloat16)
        local = jnp.dot(vectors[j], zeta[j], preferred_element_type=jnp.float32)
        at = pl.multiple_of(g * rows + j * trials, trials)
        piece[z, pl.ds(at, trials), :] = local.astype(jnp.bfloat16)
        return carry

    lax.fori_loop(0, k_local, project, 0)
    pl.semaphore_wait(barrier, len(partners))

    pending = []

    def block(group, zp):
        return piece.at[zp, pl.ds(pl.multiple_of(group * rows, rows), rows), :]

    def ag_copy(group, zp, slot, index, who):
        return pltpu.make_async_remote_copy(
            src_ref=block(group, zp),
            dst_ref=block(group, zp),
            send_sem=ag_send.at[index],
            recv_sem=ag_recv.at[slot[0], slot[1], zp],
            device_id=who,
            device_id_type=MESH,
        )

    sent = [0]

    def send(group, zp, slot, who):
        copy = ag_copy(group, zp, slot, sent[0], who)
        sent[0] += 1
        copy.start()
        pending.append(copy)

    def arrived(group, zp, slot):
        ag_copy(group, zp, slot, 0, (g, z)).wait_recv()

    order = [nearest(z, i, points) if i else z for i in range(points)]

    def forward(d, i):
        group = flip(o, d) * 2 + c
        bit = 1
        while bit < outer:
            if not d & bit and last_hop(d | bit, i, points) == bit:
                send(group, order[i], (d | bit, 0), (flip(o, bit) * 2 + c, z))
            bit *= 2
        send(group, order[i], (d, 1), (sibling, z))

    def take(d, i):
        arrived(flip(o, d) * 2 + c, order[i], (d, 0))
        forward(d, i)

    def product(d):
        base = pl.multiple_of(flip(o, d) * 2 * rows, 2 * rows)
        for i in range(points):
            arrived(flip(o, d) * 2 + 1 - c, order[i], (d, 1))

        def one(q, carry):
            lhs = jnp.concatenate([piece[t, pl.ds(base, 2 * rows), :] for t in range(points)], axis=1)
            got = lax.dot_general(
                lhs, w_buf[q], (((1,), (1,)), ((), ())), preferred_element_type=jnp.float32
            )
            res[q, pl.ds(flip(o, d) * 2 * k_local, 2 * k_local)] = got.reshape(2 * k_local, trials, m_local)
            return carry

        lax.fori_loop(0, q_local, one, 0)

    near = [d for d in range(1, outer) if d & (d - 1) == 0]
    far = [d for d in range(1, outer) if d & (d - 1)]
    far.sort(key=lambda d: bin(d).count("1"))
    for i in range(1, points):
        t = nearest(z, i, points)
        send(g, z, (0, 0), (g, t))
    forward(0, 0)
    for i in range(1, points):
        take(0, i)
        for d in near:
            take(d, i - 1)
    for d in near:
        take(d, points - 1)
    w_copy.wait()
    product(0)
    ready = near[:]
    for d in far:
        for i in range(points):
            take(d, i)
            if 2 * i + 2 == points and ready:
                product(ready.pop(0))
        while ready and d == far[-1]:
            product(ready.pop(0))
    while ready:
        product(ready.pop(0))
    for d in far:
        product(d)

    def gathered(group, j):
        k = group * k_local + j
        total = None
        for q in range(q_local):
            term = res[q, sender[q, k]]
            total = term if total is None else total + term
        return total

    first, second, third = [], [], []
    for j in range(k_local):
        for d in range(outer):
            s1[j, d] = gathered(flip(o, d) * 2 + 1 - c, j).astype(jnp.bfloat16)
        copy = pltpu.make_async_remote_copy(
            src_ref=s1.at[j], dst_ref=r1.at[j],
            send_sem=s1_send.at[j], recv_sem=s1_recv.at[j],
            device_id=(sibling, z), device_id_type=MESH,
        )
        copy.start()
        first.append(copy)
    for j in range(k_local):
        sums = [gathered(flip(o, d) * 2 + c, j) for d in range(outer)]
        first[j].wait_recv()
        mine[j] = sums[0] + r1[j, 0].astype(jnp.float32)
        copies = []
        for d in range(outer - 1, 0, -1):
            s2[j, d] = (sums[d] + r1[j, d].astype(jnp.float32)).astype(jnp.bfloat16)
            copy = pltpu.make_async_remote_copy(
                src_ref=s2.at[j, d], dst_ref=r2.at[j, d],
                send_sem=s2_send.at[j, d], recv_sem=s2_recv.at[j, d],
                device_id=(flip(o, d) * 2 + c, z), device_id_type=MESH,
            )
            copy.start()
            copies.append((d, copy))
        second.append(copies)
    for j in range(k_local):
        total = mine[j]
        for d, copy in second[j]:
            copy.wait_recv()
            total = total + r2[j, d].astype(jnp.float32)
        home = total.astype(jnp.bfloat16)

        def back(t, carry):
            at = pl.multiple_of(t * p_local, p_local)
            mine3[j, t] = lax.dot_general(
                home, zeta[j, pl.ds(at, p_local), :], (((1,), (1,)), ((), ())),
                preferred_element_type=jnp.float32,
            )
            s3[j, t] = mine3[j, t].astype(jnp.bfloat16)
            return carry

        lax.fori_loop(0, points, back, 0)
        copies = []
        for t in range(points - 1, 0, -1):
            to = (z + t) % points
            copy = pltpu.make_async_remote_copy(
                src_ref=s3.at[j, to], dst_ref=r3.at[j, t],
                send_sem=s3_send.at[j, t], recv_sem=s3_recv.at[j, t],
                device_id=(g, to), device_id_type=MESH,
            )
            copy.start()
            copies.append((t, copy))
        third.append(copies)
    for j in range(k_local):
        total = mine3[j, z]
        for t, copy in third[j]:
            copy.wait_recv()
            total = total + r3[j, t].astype(jnp.float32)
        out[j] = total.astype(jnp.bfloat16)
    for copy in pending:
        copy.wait_send()
    for j in range(k_local):
        first[j].wait_send()
        for d, copy in second[j] + third[j]:
            copy.wait_send()


def shards(
    groups, points,
    vectors, psi_val, psi_con, val_count, con_count, val_offset, con_offset, screening, q_table,
):
    k_local, trials, slots = vectors.shape
    k_total = q_table.shape[0]
    q_local, m_local, m_total = screening.shape
    outer = groups // 2
    p_local = slots // points
    rows = k_local * trials
    owned = lax.axis_index("kgrp") * q_local + jnp.arange(q_local, dtype=jnp.int32)
    match = (q_table[None, :, :] == owned[:, None, None]).astype(jnp.int32)
    sender = jnp.sum(match * jnp.arange(k_total, dtype=jnp.int32)[None, None, :], axis=2)
    sender = jnp.minimum(sender, k_total - 1)
    smem = pl.BlockSpec(memory_space=pltpu.SMEM)
    vmem = pl.BlockSpec(memory_space=pltpu.VMEM)
    bf16, f32 = jnp.bfloat16, jnp.float32
    dma = pltpu.SemaphoreType.DMA
    flops = 2 * k_total * trials * q_local * m_local * m_total
    return pl.pallas_call(
        functools.partial(kernel, groups, points),
        out_shape=jax.ShapeDtypeStruct((k_local, trials, p_local), bf16),
        in_specs=[smem] * 5 + [vmem] * 3 + [pl.BlockSpec(memory_space=pl.ANY)],
        out_specs=vmem,
        scratch_shapes=[
            pltpu.VMEM((q_local, m_local, m_total), bf16),
            pltpu.VMEM((k_local, slots, m_local), bf16),
            pltpu.VMEM((points, groups * rows, m_local), bf16),
            pltpu.VMEM((q_local, groups * k_local, trials, m_local), f32),
            pltpu.VMEM((k_local, outer, trials, m_local), bf16),
            pltpu.VMEM((k_local, outer, trials, m_local), bf16),
            pltpu.VMEM((k_local, outer, trials, m_local), bf16),
            pltpu.VMEM((k_local, outer, trials, m_local), bf16),
            pltpu.VMEM((k_local, trials, m_local), f32),
            pltpu.VMEM((k_local, points, trials, p_local), bf16),
            pltpu.VMEM((k_local, points, trials, p_local), bf16),
            pltpu.VMEM((k_local, points, trials, p_local), f32),
            dma,
            dma((groups * points,)),
            dma((outer, 2, points)),
            dma((k_local,)),
            dma((k_local,)),
            dma((k_local, outer)),
            dma((k_local, outer)),
            dma((k_local, points)),
            dma((k_local, points)),
        ],
        compiler_params=pltpu.CompilerParams(
            collective_id=0, has_side_effects=True, vmem_limit_bytes=VMEM_BYTES
        ),
        cost_estimate=pl.CostEstimate(flops=flops, bytes_accessed=screening.size * 2, transcendentals=0),
    )(
        val_count, con_count, val_offset, con_offset, sender,
        vectors, psi_val, psi_con, screening,
    )


def solution(mesh):
    placed = (
        P("kgrp", None, None),
        P("kgrp", None, "pts"),
        P("kgrp", None, "pts"),
        P("kgrp"),
        P("kgrp"),
        P("kgrp"),
        P("kgrp"),
        P("kgrp", "pts", None),
        P(),
    )
    return jax.shard_map(
        functools.partial(shards, mesh.shape["kgrp"], mesh.shape["pts"]),
        mesh=mesh, in_specs=placed, out_specs=P("kgrp", None, "pts"), check_vma=False,
    )
```

time: 196 us -> 64.6 us (0.33)
  waiting for transfers between devices: 96.6 us -> 0 us
  Pallas kernels: 0 us -> 61.2 us
  matrix products: 30.2 us -> 0 us
  local copies, waits for them, and re-layouts: 28.5 us -> 1.57 us
  blocking collectives: 18 us -> 0 us
  between operations: 13.3 us -> 0.01 us
  other arithmetic: 8.77 us -> 1.52 us
    pallas_call x0 -> x1, Pallas kernels: none -> 61.2 us  [shards(): pl.pallas_call(functools.partial(kernel, groups, points), out_shape=jax.S...]
    reduce_scatter x2 -> x0, waiting for transfers between devices: 57.9 us -> none  [the longest x1 36.1 us: shards(): lax.psum_scatter(summed.astype(jnp.bfloat16), 'kgrp', scatter_dimension=0...]
    all_gather x1 -> x0, waiting for transfers between devices: 38.7 us -> none  [shards(): piece = lax.all_gather(spread, 'kgrp', axis=0, tiled=True)]
    dot_general x6 -> x0, matrix products: 30.2 us -> none  [the longest x4 21.9 us: one_transfer(): jnp.einsum('cbv,mv->cbm', picked, q_block, preferred_element_type=jnp.flo...]
    gather x6 -> x0, local copies, waits for them, and re-layouts: 22.7 us -> none  [the longest x4 19.8 us: one_transfer(): jnp.take(piece, sender_kpoint, axis=0)]
    all_gather x1 -> x0, blocking collectives: 18 us -> none  [shards(): spread = lax.all_gather(local, 'pts', axis=2, tiled=True)]
    convert_element_type x8 -> x0, other arithmetic: 5.13 us -> none  [the longest x1 3.25 us: pair_window(): return prod.reshape(NV * NC, prod.shape[-1]).astype(jnp.bfloat16)]
    dynamic_slice x4 -> x0, local copies, waits for them, and re-layouts: 2.22 us -> none  [shards(): summed, unused_slot = lax.scan(one_transfer, empty, (owned, screening))]
  transfers between devices with their start and end apart: 3 -> 0, of which waited for: 3 -> 0; matrix products, arithmetic and copies ran while one was open for 0% -> 0% of each run, Pallas kernels for 0% -> 0%
where the time goes in v1:
time: 64.6 us; the launch traced here: 64.3 us
  Pallas kernels  61.2 us (95%)
  local copies, waits for them, and re-layouts  1.57 us (2%)
  other arithmetic  1.52 us (2%)
    pallas_call x1, Pallas kernels, shards(): pl.pallas_call(functools.partial(kernel, groups, points), out_shape=jax.S...  61.2 us
    unnamed x1, local copies, waits for them, and re-layouts  1.57 us

profile of v1, /device:TPU:0, one launch (start us, length us, event | category | flops | bytes accessed | tf_op | source)
XLA Modules:
  0.0 64.3 jit_solution(2559467568700569413)
XLA Ops:
  0.0 0.9 %select_reduce_fusion = s32[4,32]{1,0:T(4,128)S(1)} fusion(s32[32,32]{1,0:T(8,128)} %param.17, s32[4]{0:T(128)S(1)} %iota_add_fusion), kind=kLoop, calls=%fused_computation | loop fusion | flops 12160 | bytes 4624 | tf_op jit(solution)/shard_map/reduce_sum | solution.py:266
  0.9 0.6 broadcast_minimum_fusion.sender
  1.5 61.2 %shard_map.91 = bf16[4,32,512]{2,1,0:T(8,128)(2,1)} custom-call(s32[4]{0:T(128)} %val_count.1, s32[4]{0:T(128)} %con_count.1, s32[4]{0:T(128)} %val_offset.1, s32[4]{0:T(128)} %con_offset.1, s32[4,32]{1,0:T(4,128)} %broadcast_minimum_fusion.sender, bf16[4,32,2048]{2,1,0:T(8,128)(2,1)} %vectors.1, bf16[4,48,512]{2,1,0:T(8,128)(2,1)} %psi_val.1, ...), custom_call_target="tpu_custom_call" | custom-call | flops 8589934592 | bytes 8388608 | tf_op jit(solution)/shard_map/pallas_call | solution.py:273
  62.8 1.6 %copy.11 = bf16[4,32,512]{2,1,0:T(8,128)(2,1)} copy(bf16[4,32,512]{2,1,0:T(8,128)(2,1)} %shard_map.91) | data formatting | bytes 262144
  (1 shorter events, 0.0 us)

commit v2 on v1

--- a/solution.py
+++ b/solution.py
@@ -37,7 +37,7 @@
 
 
 def kernel(
-    groups, points,
+    groups, points, halves,
     val_count, con_count, val_offset, con_offset, sender,
     vectors, psi_val, psi_con, screening, out,
     w_buf, zeta, piece, res, s1, r1, s2, r2, mine, s3, r3, mine3,
@@ -64,8 +64,6 @@
     w_copy = pltpu.make_async_copy(screening, w_buf, w_sem)
     w_copy.start()
 
-    my_rows = pl.multiple_of(g * rows, rows)
-
     def project(j, carry):
         def select(count, offset, n, held):
             at = lax.broadcasted_iota(jnp.int32, (n, held), 0)
@@ -88,20 +86,19 @@
         piece[z, pl.ds(at, trials), :] = local.astype(jnp.bfloat16)
         return carry
 
-    lax.fori_loop(0, k_local, project, 0)
-    pl.semaphore_wait(barrier, len(partners))
-
     pending = []
 
-    def block(group, zp):
-        return piece.at[zp, pl.ds(pl.multiple_of(group * rows, rows), rows), :]
+    part = rows // halves
+
+    def block(group, zp, h):
+        return piece.at[zp, pl.ds(pl.multiple_of(group * rows + h * part, part), part), :]
 
     def ag_copy(group, zp, slot, index, who):
         return pltpu.make_async_remote_copy(
-            src_ref=block(group, zp),
-            dst_ref=block(group, zp),
+            src_ref=block(group, zp, slot[2]),
+            dst_ref=block(group, zp, slot[2]),
             send_sem=ag_send.at[index],
-            recv_sem=ag_recv.at[slot[0], slot[1], zp],
+            recv_sem=ag_recv.at[slot[0], slot[1], slot[2], zp],
             device_id=who,
             device_id_type=MESH,
         )
@@ -119,23 +116,24 @@
 
     order = [nearest(z, i, points) if i else z for i in range(points)]
 
-    def forward(d, i):
+    def forward(d, i, h):
         group = flip(o, d) * 2 + c
         bit = 1
         while bit < outer:
             if not d & bit and last_hop(d | bit, i, points) == bit:
-                send(group, order[i], (d | bit, 0), (flip(o, bit) * 2 + c, z))
+                send(group, order[i], (d | bit, 0, h), (flip(o, bit) * 2 + c, z))
             bit *= 2
-        send(group, order[i], (d, 1), (sibling, z))
-
-    def take(d, i):
-        arrived(flip(o, d) * 2 + c, order[i], (d, 0))
-        forward(d, i)
+        send(group, order[i], (d, 1, h), (sibling, z))
+
+    def take(d, i, h):
+        arrived(flip(o, d) * 2 + c, order[i], (d, 0, h))
+        forward(d, i, h)
 
     def product(d):
         base = pl.multiple_of(flip(o, d) * 2 * rows, 2 * rows)
         for i in range(points):
-            arrived(flip(o, d) * 2 + 1 - c, order[i], (d, 1))
+            for h in range(halves):
+                arrived(flip(o, d) * 2 + 1 - c, order[i], (d, 1, h))
 
         def one(q, carry):
             lhs = jnp.concatenate([piece[t, pl.ds(base, 2 * rows), :] for t in range(points)], axis=1)
@@ -150,26 +148,29 @@
     near = [d for d in range(1, outer) if d & (d - 1) == 0]
     far = [d for d in range(1, outer) if d & (d - 1)]
     far.sort(key=lambda d: bin(d).count("1"))
-    for i in range(1, points):
-        t = nearest(z, i, points)
-        send(g, z, (0, 0), (g, t))
-    forward(0, 0)
-    for i in range(1, points):
-        take(0, i)
-        for d in near:
-            take(d, i - 1)
-    for d in near:
-        take(d, points - 1)
+    each = k_local // halves
+    for h in range(halves):
+        lax.fori_loop(h * each, (h + 1) * each, project, 0)
+        if h == 0:
+            pl.semaphore_wait(barrier, len(partners))
+        for i in range(1, points):
+            send(g, z, (0, 0, h), (g, order[i]))
+        forward(0, 0, h)
+    expected = [(i + 1.5 * h, 0, i, h) for h in range(halves) for i in range(1, points)]
+    expected += [
+        (i + 1.5 * h + 0.9, d, i, h) for h in range(halves) for i in range(points) for d in near
+    ]
+    for when, d, i, h in sorted(expected):
+        take(d, i, h)
     w_copy.wait()
     product(0)
     ready = near[:]
     for d in far:
-        for i in range(points):
-            take(d, i)
-            if 2 * i + 2 == points and ready:
+        for h in range(halves):
+            for i in range(points):
+                take(d, i, h)
+            if h == 0 and ready:
                 product(ready.pop(0))
-        while ready and d == far[-1]:
-            product(ready.pop(0))
     while ready:
         product(ready.pop(0))
     for d in far:
@@ -261,17 +262,17 @@
     outer = groups // 2
     p_local = slots // points
     rows = k_local * trials
+    halves = 1 if k_local % 2 else 2
     owned = lax.axis_index("kgrp") * q_local + jnp.arange(q_local, dtype=jnp.int32)
     match = (q_table[None, :, :] == owned[:, None, None]).astype(jnp.int32)
     sender = jnp.sum(match * jnp.arange(k_total, dtype=jnp.int32)[None, None, :], axis=2)
-    sender = jnp.minimum(sender, k_total - 1)
     smem = pl.BlockSpec(memory_space=pltpu.SMEM)
     vmem = pl.BlockSpec(memory_space=pltpu.VMEM)
     bf16, f32 = jnp.bfloat16, jnp.float32
     dma = pltpu.SemaphoreType.DMA
     flops = 2 * k_total * trials * q_local * m_local * m_total
     return pl.pallas_call(
-        functools.partial(kernel, groups, points),
+        functools.partial(kernel, groups, points, halves),
         out_shape=jax.ShapeDtypeStruct((k_local, trials, p_local), bf16),
         in_specs=[smem] * 5 + [vmem] * 3 + [pl.BlockSpec(memory_space=pl.ANY)],
         out_specs=vmem,
@@ -289,8 +290,8 @@
             pltpu.VMEM((k_local, points, trials, p_local), bf16),
             pltpu.VMEM((k_local, points, trials, p_local), f32),
             dma,
-            dma((groups * points,)),
-            dma((outer, 2, points)),
+            dma((groups * points * halves,)),
+            dma((outer, 2, halves, points)),
             dma((k_local,)),
             dma((k_local,)),
             dma((k_local, outer)),

time: 64.6 us -> 68.5 us (1.060)
  Pallas kernels: 61.2 us -> 65.2 us
    pallas_call x1, Pallas kernels: 61.2 us -> 65.2 us  [shards(): pl.pallas_call(functools.partial(kernel, groups, points, halves), out_sha...]
where the time goes in v2:
time: 68.5 us; the launch traced here: 68.3 us
  Pallas kernels  65.2 us (95%)
  local copies, waits for them, and re-layouts  1.57 us (2%)
  other arithmetic  1.51 us (2%)
    pallas_call x1, Pallas kernels, shards(): pl.pallas_call(functools.partial(kernel, groups, points, halves), out_sha...  65.2 us
    unnamed x1, local copies, waits for them, and re-layouts  1.57 us
    reduce_sum x1, other arithmetic, shards(): jnp.sum(match * jnp.arange(k_total, dtype=jnp.int32)[None, None, :], axis=2)  1.51 us

profile of v2, /device:TPU:0, one launch (start us, length us, event | category | flops | bytes accessed | tf_op | source)
XLA Modules:
  0.0 68.3 jit_solution(9505500107349551337)
XLA Ops:
  0.0 1.5 %select_reduce_fusion.sender = s32[4,32]{1,0:T(4,128)} fusion(s32[32,32]{1,0:T(8,128)} %param.17, s32[4]{0:T(128)S(1)} %iota_add_fusion), kind=kLoop, calls=%fused_computation | loop fusion | flops 12160 | bytes 4624 | tf_op jit(solution)/shard_map/reduce_sum | solution.py:268
  1.5 65.2 %shard_map.91 = bf16[4,32,512]{2,1,0:T(8,128)(2,1)} custom-call(s32[4]{0:T(128)} %val_count.1, s32[4]{0:T(128)} %con_count.1, s32[4]{0:T(128)} %val_offset.1, s32[4]{0:T(128)} %con_offset.1, s32[4,32]{1,0:T(4,128)} %select_reduce_fusion.sender, bf16[4,32,2048]{2,1,0:T(8,128)(2,1)} %vectors.1, bf16[4,48,512]{2,1,0:T(8,128)(2,1)} %psi_val.1, ...), custom_call_target="tpu_custom_call" | custom-call | flops 8589934592 | bytes 8388608 | tf_op jit(solution)/shard_map/pallas_call | solution.py:274
  66.7 1.6 %copy.11 = bf16[4,32,512]{2,1,0:T(8,128)(2,1)} copy(bf16[4,32,512]{2,1,0:T(8,128)(2,1)} %shard_map.91) | data formatting | bytes 262144
  (1 shorter events, 0.0 us)

commit v3 on v1

--- a/solution.py
+++ b/solution.py
@@ -183,10 +183,12 @@
             total = term if total is None else total + term
         return total
 
+    batches, each = mine.shape[0], mine.shape[1]
     first, second, third = [], [], []
-    for j in range(k_local):
+    for j in range(batches):
         for d in range(outer):
-            s1[j, d] = gathered(flip(o, d) * 2 + 1 - c, j).astype(jnp.bfloat16)
+            for e in range(each):
+                s1[j, d, e] = gathered(flip(o, d) * 2 + 1 - c, j * each + e).astype(jnp.bfloat16)
         copy = pltpu.make_async_remote_copy(
             src_ref=s1.at[j], dst_ref=r1.at[j],
             send_sem=s1_send.at[j], recv_sem=s1_recv.at[j],
@@ -194,13 +196,15 @@
         )
         copy.start()
         first.append(copy)
-    for j in range(k_local):
-        sums = [gathered(flip(o, d) * 2 + c, j) for d in range(outer)]
+    for j in range(batches):
         first[j].wait_recv()
-        mine[j] = sums[0] + r1[j, 0].astype(jnp.float32)
+        for e in range(each):
+            mine[j, e] = gathered(g, j * each + e) + r1[j, 0, e].astype(jnp.float32)
         copies = []
         for d in range(outer - 1, 0, -1):
-            s2[j, d] = (sums[d] + r1[j, d].astype(jnp.float32)).astype(jnp.bfloat16)
+            for e in range(each):
+                own = gathered(flip(o, d) * 2 + c, j * each + e)
+                s2[j, d, e] = (own + r1[j, d, e].astype(jnp.float32)).astype(jnp.bfloat16)
             copy = pltpu.make_async_remote_copy(
                 src_ref=s2.at[j, d], dst_ref=r2.at[j, d],
                 send_sem=s2_send.at[j, d], recv_sem=s2_recv.at[j, d],
@@ -209,7 +213,7 @@
             copy.start()
             copies.append((d, copy))
         second.append(copies)
-    for j in range(k_local):
+    for j in range(batches):
         total = mine[j]
         for d, copy in second[j]:
             copy.wait_recv()
@@ -218,11 +222,13 @@
 
         def back(t, carry):
             at = pl.multiple_of(t * p_local, p_local)
-            mine3[j, t] = lax.dot_general(
-                home, zeta[j, pl.ds(at, p_local), :], (((1,), (1,)), ((), ())),
-                preferred_element_type=jnp.float32,
-            )
-            s3[j, t] = mine3[j, t].astype(jnp.bfloat16)
+            for e in range(each):
+                got = lax.dot_general(
+                    home[e], zeta[j * each + e, pl.ds(at, p_local), :], (((1,), (1,)), ((), ())),
+                    preferred_element_type=jnp.float32,
+                )
+                mine3[j, t, e] = got
+                s3[j, t, e] = got.astype(jnp.bfloat16)
             return carry
 
         lax.fori_loop(0, points, back, 0)
@@ -237,15 +243,15 @@
             copy.start()
             copies.append((t, copy))
         third.append(copies)
-    for j in range(k_local):
+    for j in range(batches):
         total = mine3[j, z]
         for t, copy in third[j]:
             copy.wait_recv()
             total = total + r3[j, t].astype(jnp.float32)
-        out[j] = total.astype(jnp.bfloat16)
+        out[j * each : (j + 1) * each] = total.astype(jnp.bfloat16)
     for copy in pending:
         copy.wait_send()
-    for j in range(k_local):
+    for j in range(batches):
         first[j].wait_send()
         for d, copy in second[j] + third[j]:
             copy.wait_send()
@@ -261,6 +267,8 @@
     outer = groups // 2
     p_local = slots // points
     rows = k_local * trials
+    batches = 1 if k_local % 2 else 2
+    each = k_local // batches
     owned = lax.axis_index("kgrp") * q_local + jnp.arange(q_local, dtype=jnp.int32)
     match = (q_table[None, :, :] == owned[:, None, None]).astype(jnp.int32)
     sender = jnp.sum(match * jnp.arange(k_total, dtype=jnp.int32)[None, None, :], axis=2)
@@ -280,14 +288,14 @@
             pltpu.VMEM((k_local, slots, m_local), bf16),
             pltpu.VMEM((points, groups * rows, m_local), bf16),
             pltpu.VMEM((q_local, groups * k_local, trials, m_local), f32),
-            pltpu.VMEM((k_local, outer, trials, m_local), bf16),
-            pltpu.VMEM((k_local, outer, trials, m_local), bf16),
-            pltpu.VMEM((k_local, outer, trials, m_local), bf16),
-            pltpu.VMEM((k_local, outer, trials, m_local), bf16),
-            pltpu.VMEM((k_local, trials, m_local), f32),
-            pltpu.VMEM((k_local, points, trials, p_local), bf16),
-            pltpu.VMEM((k_local, points, trials, p_local), bf16),
-            pltpu.VMEM((k_local, points, trials, p_local), f32),
+            pltpu.VMEM((batches, outer, each, trials, m_local), bf16),
+            pltpu.VMEM((batches, outer, each, trials, m_local), bf16),
+            pltpu.VMEM((batches, outer, each, trials, m_local), bf16),
+            pltpu.VMEM((batches, outer, each, trials, m_local), bf16),
+            pltpu.VMEM((batches, each, trials, m_local), f32),
+            pltpu.VMEM((batches, points, each, trials, p_local), bf16),
+            pltpu.VMEM((batches, points, each, trials, p_local), bf16),
+            pltpu.VMEM((batches, points, each, trials, p_local), f32),
             dma,
             dma((groups * points,)),
             dma((outer, 2, points)),

time: 64.6 us -> 66.9 us (1.036)
  Pallas kernels: 61.2 us -> 63.6 us
    pallas_call x1, Pallas kernels: 61.2 us -> 63.6 us  [shards(): pl.pallas_call(functools.partial(kernel, groups, points), out_shape=jax.S...]
where the time goes in v3:
time: 66.9 us; the launch traced here: 66.7 us
  Pallas kernels  63.6 us (95%)
  local copies, waits for them, and re-layouts  1.57 us (2%)
  other arithmetic  1.52 us (2%)
    pallas_call x1, Pallas kernels, shards(): pl.pallas_call(functools.partial(kernel, groups, points), out_shape=jax.S...  63.6 us
    unnamed x1, local copies, waits for them, and re-layouts  1.57 us

profile of v3, /device:TPU:0, one launch (start us, length us, event | category | flops | bytes accessed | tf_op | source)
XLA Modules:
  0.0 66.7 jit_solution(16270667338517157863)
XLA Ops:
  0.0 0.9 %select_reduce_fusion = s32[4,32]{1,0:T(4,128)S(1)} fusion(s32[32,32]{1,0:T(8,128)} %param.17, s32[4]{0:T(128)S(1)} %iota_add_fusion), kind=kLoop, calls=%fused_computation | loop fusion | flops 12160 | bytes 4624 | tf_op jit(solution)/shard_map/reduce_sum | solution.py:274
  0.9 0.6 broadcast_minimum_fusion.sender
  1.5 63.6 %shard_map.91 = bf16[4,32,512]{2,1,0:T(8,128)(2,1)} custom-call(s32[4]{0:T(128)} %val_count.1, s32[4]{0:T(128)} %con_count.1, s32[4]{0:T(128)} %val_offset.1, s32[4]{0:T(128)} %con_offset.1, s32[4,32]{1,0:T(4,128)} %broadcast_minimum_fusion.sender, bf16[4,32,2048]{2,1,0:T(8,128)(2,1)} %vectors.1, bf16[4,48,512]{2,1,0:T(8,128)(2,1)} %psi_val.1, ...), custom_call_target="tpu_custom_call" | custom-call | flops 8589934592 | bytes 8388608 | tf_op jit(solution)/shard_map/pallas_call | solution.py:281
  65.1 1.6 %copy.11 = bf16[4,32,512]{2,1,0:T(8,128)(2,1)} copy(bf16[4,32,512]{2,1,0:T(8,128)(2,1)} %shard_map.91) | data formatting | bytes 262144
  (1 shorter events, 0.0 us)
